TPU v7x, 32 devices: a whole 2x2x4 slice. The times are simulated.
32 devices in a mesh: ctx: 8 (over z, x), tp: 4 (over y, core).
Axes of the slice: x: 2, y: 2, z: 4, core: 2. Of those that a mesh axis runs over, the one named last changes fastest.
Arguments:
- tokens_in: bfloat16 [4096, 2048], P('ctx'), may hold values from -6 to 6
- w_query: bfloat16 [2048, 2048], P(None, 'tp'), may hold values from -0.125 to 0.125
- w_key: bfloat16 [2048, 2048], P(None, 'tp'), may hold values from -0.125 to 0.125
- w_value: bfloat16 [2048, 2048], P(None, 'tp'), may hold values from -0.125 to 0.125
- grad_out: bfloat16 [4096, 2048], P('ctx', 'tp'), may hold values from -4 to 4
- trajectory_ends: int32 [4096], P('ctx'), may hold values from 0 to 1, as said below
Outputs:
- grad_tokens: bfloat16 [4096, 2048], P(('ctx', 'tp'))
Inputs may be any that keep to these rules, and one draw needn't show every extreme that they name: `trajectory_ends`: 1 marks a token that ends a trajectory, 0 any other token; trajectories may span many blocks.
All inputs are finite; a program needn't handle non-finite values.
Results may differ from a plain program's by a relative error of at most 0.0061.
Values sent between devices are 32-bit elements; how exact they have to be, the bound alone decides.
A program may use at most 128 MiB of HBM per device.

v0:
```python
import jax
import jax.numpy as jnp
from jax import lax
from jax.sharding import PartitionSpec as P

HD = 128


def prefix(part, axis, combine, identity):
    count = lax.axis_size(axis)
    place = lax.axis_index(axis)
    ahead = count - 1 - place
    gathered = jax.tree.map(lambda a: lax.all_gather(a, axis), part)
    state = jax.tree.map(lambda a, e: jnp.zeros_like(a) + jnp.asarray(e, a.dtype), part, identity)

    def one(hop, state):
        source = count - 1 - hop
        return combine(
            state, jax.tree.map(lambda a: lax.dynamic_index_in_dim(a, source, 0, False), gathered)
        )

    return lax.fori_loop(0, ahead, one, state)


def joined(earlier, later):
    return (later[0] + (1.0 - later[1][0]) * earlier[0], jnp.maximum(earlier[1], later[1]))


def body(tokens_in, w_query, w_key, w_value, grad_out, trajectory_ends):
    row_count = tokens_in.shape[0]
    head_count = w_query.shape[1] // HD
    shape = (row_count, head_count, HD)
    queries = (
        jnp.dot(tokens_in, w_query, preferred_element_type=jnp.float32)
        .astype(jnp.bfloat16)
        .reshape(shape)
    )
    key_rows = (
        jnp.dot(tokens_in, w_key, preferred_element_type=jnp.float32)
        .astype(jnp.bfloat16)
        .reshape(shape)
    )
    value_rows = (
        jnp.dot(tokens_in, w_value, preferred_element_type=jnp.float32)
        .astype(jnp.bfloat16)
        .reshape(shape)
    )
    grad_rows = grad_out.reshape(shape)
    before = jnp.cumsum(trajectory_ends) - trajectory_ends
    end_total = jnp.sum(trajectory_ends)
    opened = before == 0
    closed = end_total - before == 0
    positions = jnp.arange(row_count, dtype=jnp.int32)
    pair_mask = (positions[None, :] <= positions[:, None]) & (before[:, None] == before[None, :])
    reset_any = (end_total > 0).astype(jnp.float32).reshape(1)
    open_bf = opened.astype(jnp.bfloat16)[:, None, None]
    close_bf = closed.astype(jnp.bfloat16)[:, None, None]
    carry_out = jnp.einsum(
        "shv,shk->hvk", value_rows * close_bf, key_rows, preferred_element_type=jnp.float32
    )
    grads_out = jnp.einsum(
        "thv,thk->hvk", grad_rows * open_bf, queries, preferred_element_type=jnp.float32
    )
    zero_state = jnp.zeros((head_count, HD, HD), jnp.float32)
    zero_flag = jnp.zeros((1,), jnp.float32)
    flag_list = lax.all_gather(reset_any, "ctx", axis=0, tiled=True)
    own_index = lax.axis_index("ctx")
    order = jnp.arange(flag_list.shape[0], dtype=jnp.int32)
    start_from = jnp.max(jnp.where((order < own_index) & (flag_list > 0), order, 0))
    piece = lax.all_gather(carry_out[None], "ctx", axis=0, tiled=True)
    index_list = jnp.arange(piece.shape[0], dtype=jnp.int32)
    weights = ((index_list >= start_from) & (index_list < own_index)).astype(jnp.float32)
    state_in = jnp.sum(weights[:, None, None, None] * piece, axis=0)
    grads_in = prefix((grads_out, reset_any), "ctx", joined, (zero_state, zero_flag))[0]
    scores = jnp.einsum("thv,shv->hts", grad_rows, value_rows, preferred_element_type=jnp.float32)
    scores = jnp.where(pair_mask[None], scores, 0.0).astype(jnp.bfloat16)
    attn = jnp.einsum("thk,shk->hts", queries, key_rows, preferred_element_type=jnp.float32)
    attn = jnp.where(pair_mask[None], attn, 0.0).astype(jnp.bfloat16)
    state_bf = state_in.astype(jnp.bfloat16)
    grads_bf = grads_in.astype(jnp.bfloat16)
    open_f = opened.astype(jnp.float32)[:, None, None]
    close_f = closed.astype(jnp.float32)[:, None, None]
    score_scale = 1.0 / HD
    grad_query = jnp.einsum("hts,shk->thk", scores, key_rows, preferred_element_type=jnp.float32)
    grad_query = grad_query + open_f * jnp.einsum(
        "thv,hvk->thk", grad_rows, state_bf, preferred_element_type=jnp.float32
    )
    grad_key = jnp.einsum("hts,thk->shk", scores, queries, preferred_element_type=jnp.float32)
    grad_key = grad_key + close_f * jnp.einsum(
        "shv,hvk->shk", value_rows, grads_bf, preferred_element_type=jnp.float32
    )
    grad_value = jnp.einsum("hts,thv->shv", attn, grad_rows, preferred_element_type=jnp.float32)
    grad_value = grad_value + close_f * jnp.einsum(
        "shk,hvk->shv", key_rows, grads_bf, preferred_element_type=jnp.float32
    )
    flat = (row_count, head_count * HD)
    grad_query = (score_scale * grad_query).astype(jnp.bfloat16).reshape(flat)
    grad_key = (score_scale * grad_key).astype(jnp.bfloat16).reshape(flat)
    grad_value = (score_scale * grad_value).astype(jnp.bfloat16).reshape(flat)
    dims = (((1,), (1,)), ((), ()))
    total = lax.dot_general(grad_query, w_query, dims, preferred_element_type=jnp.float32)
    total = total + lax.dot_general(grad_key, w_key, dims, preferred_element_type=jnp.float32)
    total = total + lax.dot_general(grad_value, w_value, dims, preferred_element_type=jnp.float32)
    shares = lax.psum_scatter(total, "tp", scatter_dimension=0, tiled=True)
    return shares.astype(jnp.bfloat16)


def solution(mesh):
    return jax.shard_map(
        body,
        mesh=mesh,
        in_specs=(
            P("ctx", None),
            P(None, "tp"),
            P(None, "tp"),
            P(None, "tp"),
            P("ctx", "tp"),
            P("ctx"),
        ),
        out_specs=P(("ctx", "tp"), None),
        check_vma=False,
    )
```

profile of v0, /device:TPU:0, one launch (start us, length us, event | category | flops | bytes accessed | tf_op | source)
XLA Modules:
  0.0 177.2 jit_solution(295720408558832032)
XLA Ops:
  6.5 1.1 reduce-window.9
  8.7 1.3 copy.63
  9.9 3.5 %convolution_convert_fusion = bf16[512,512]{0,1:T(8,128)(2,1)S(1)} fusion(bf16[512,2048]{1,0:T(8,128)(2,1)} %param.8, bf16[2048,512]{1,0:T(8,128)(2,1)} %param.9), kind=kOutput, calls=%fused_computation.19 | convolution fusion | flops 1074003968 | bytes 4718592 | tf_op jit(solution)/shard_map/dot_general | solution.py:34
  13.5 1.0 fusion.14
  15.8 3.0 %convolution_convert_fusion.2 = bf16[512,512]{0,1:T(8,128)(2,1)S(1)} fusion(bf16[512,2048]{1,0:T(8,128)(2,1)} %param.8, bf16[2048,512]{1,0:T(8,128)(2,1)S(1)} %copy-done), kind=kOutput, calls=%fused_computation.21 | convolution fusion | flops 1074003968 | bytes 4718592 | tf_op jit(solution)/shard_map/dot_general | solution.py:39
  18.8 1.3 convolution_convert_fusion.1
  20.2 0.8 copy-done.6
  20.9 1.0 fusion.16
  23.9 23.2 %all-reduce = f32[8]{0:T(128)S(1)} all-reduce(f32[8]{0:T(128)S(1)} %dynamic-update-slice), channel_id=1, replica_groups=mesh['ctx'=8,'tp'=4] {'ctx'}, use_global_device_ids=true, to_apply=%add | all-reduce | flops 8 | bytes 64
  48.5 2.0 %fusion = bf16[4,512,512]{1,2,0:T(8,128)(2,1)S(1)} fusion(bf16[512,4,128]{0,2,1:T(8,128)(2,1)} %bitcast.83, bf16[512,4,128]{0,2,1:T(8,128)(2,1)S(1)} %bitcast.69, pred[512,512]{0,1:T(8,128)(4,1)S(1)} %fusion.13), kind=kOutput, calls=%fused_computation.3 | convolution fusion | flops 270532608 | bytes 3407872 | tf_op jit(solution)/shard_map/thv,shv->hts/dot_general | solution.py:75
  50.5 1.8 %fusion.30 = f32[4,128,512]{2,1,0:T(8,128)} fusion(bf16[512,4,128]{0,2,1:T(8,128)(2,1)S(1)} %bitcast.80, bf16[4,512,512]{1,2,0:T(8,128)(2,1)S(1)} %fusion), kind=kOutput, calls=%fused_computation.49 | convolution fusion | flops 268435456 | bytes 3670016 | tf_op jit(solution)/shard_map/hts,thk->shk/dot_general | solution.py:88
  52.3 1.4 fusion.28
  53.7 13.1 %all-gather.7.cloned.1.call-done = f32[32,128,128]{2,1,0:T(8,128)} async-done(((f32[4,128,128]{2,1,0:T(8,128)}), f32[32,128,128]{2,1,0:T(8,128)}) %all-gather.7.cloned.1.call-update) | async-done | bytes 2097168 | tf_op jit(solution)/shard_map/all_gather | solution.py:13
  66.8 15.4 %while.14 = (s32[]{:T(128)}, f32[4,128,128]{2,1,0:T(8,128)S(1)}, s32[]{:T(128)}, f32[8,4,128,128]{3,2,1,0:T(8,128)}, f32[8,1]{0,1:T(1,128)S(1)}, /*index=5*/s32[]{:T(128)}, s32[]{:T(128)}, s32[]{:T(128)}, s32[]{:T(128)}) while((s32[]{:T(128)}, f32[4,128,128]{2,1,0:T(8,128)S(1)}, s32[]{:T(128)}, f32[8,4,128,128]{3,2,1,0:T(8,128)}, ...), condition=%wide.region_6.7_spmd, body=%wide.region_5.6_spmd.sunk | while | flops 131079 | bytes 786599 | solution.py:22
  67.3 1.6 bitcast_add_fusion.2
  69.5 1.6 bitcast_add_fusion.2
  71.7 1.6 bitcast_add_fusion.2
  73.9 1.6 bitcast_add_fusion.2
  76.1 1.6 bitcast_add_fusion.2
  78.2 1.6 bitcast_add_fusion.2
  80.4 1.6 bitcast_add_fusion.2
  82.2 1.3 fusion.5
  83.9 1.1 fusion.11
  85.1 3.7 %fusion.12 = bf16[512,4,128]{0,2,1:T(8,128)(2,1)} fusion(f32[512,4,128]{0,2,1:T(8,128)} %fusion.5, bf16[512,4,128]{0,2,1:T(8,128)(2,1)S(1)} %bitcast.70, bf16[512,4,128]{0,2,1:T(8,128)(2,1)} %bitcast.79, bf16[512,4,128]{0,2,1:T(8,128)(2,1)S(1)} %bitcast.75, pred[512,512]{0,1:T(8,128)(4,1)} %copy-done.12), kind=kOutput, calls=%fused_computation.24 | convolution fusion | flops 539754496 | bytes 3407872 | tf_op jit(solution)/shard_map/hts,thv->shv/dot_general | solution.py:92
  88.8 4.3 %fusion.31 = f32[512,2048]{1,0:T(8,128)} fusion(bf16[512,512]{0,1:T(8,128)(2,1)} %bitcast.77, bf16[2048,512]{1,0:T(8,128)(2,1)S(1)} %copy-done), kind=kOutput, calls=%fused_computation.50 | convolution fusion | flops 1073741824 | bytes 6815744 | tf_op jit(solution)/shard_map/dot_general | solution.py:102
  93.1 23.6 %all-gather.5.cloned.1.call-done = f32[32,128,128]{2,1,0:T(8,128)} async-done(((f32[4,128,128]{2,1,0:T(8,128)}), f32[32,128,128]{2,1,0:T(8,128)}) %all-gather.5.cloned.1.call-update) | async-done | bytes 2097168 | tf_op jit(solution)/shard_map/all_gather | solution.py:70
  116.7 2.0 %multiply_reduce_fusion = bf16[4,128,128]{2,1,0:T(8,128)(2,1)S(1)} fusion(f32[8,4,128,128]{3,2,1,0:T(8,128)} %bitcast.81, f32[8]{0:T(128)S(1)} %and_convert_fusion), kind=kLoop, calls=%fused_computation.6 | loop fusion | flops 983040 | bytes 2228256 | tf_op jit(solution)/shard_map/reduce_sum | solution.py:73
  119.2 1.3 fusion.29
  120.5 0.9 copy-done.1
  122.1 3.3 %add_add_fusion = f32[512,2048]{1,0:T(8,128)} fusion(f32[512,2048]{1,0:T(8,128)S(1)} %fusion.29, f32[512,2048]{1,0:T(8,128)S(1)} %copy-done.1, bf16[512,512]{0,1:T(8,128)(2,1)S(1)} %bitcast.86, bf16[2048,512]{1,0:T(8,128)(2,1)S(1)} %copy-done.10), kind=kOutput, calls=%fused_computation.5 | convolution fusion | flops 1075838976 | bytes 15204352 | tf_op jit(solution)/shard_map/dot_general | solution.py:103
  125.5 43.1 %reduce-scatter.2.cloned.1.call-done = f32[128,2048]{1,0:T(8,128)} async-done(((f32[512,2048]{1,0:T(8,128)}), f32[128,2048]{1,0:T(8,128)}) %reduce-scatter.2.cloned.1.call-update) | async-done | bytes 1048592 | tf_op jit(solution)/shard_map/reduce_scatter | solution.py:104
  168.6 2.1 %convert_element_type.79 = bf16[128,2048]{1,0:T(8,128)(2,1)} convert(f32[128,2048]{1,0:T(8,128)} %reduce-scatter.2.cloned.1.call-done) | non-fusion elementwise | flops 262144 | bytes 1572864 | tf_op jit(solution)/shard_map/convert_element_type | solution.py:105
  (59 shorter events, 10.6 us)
Async XLA Ops:
  6.5 9.2 %copy-start = (bf16[2048,512]{1,0:T(8,128)(2,1)S(1)}, bf16[2048,512]{1,0:T(8,128)(2,1)}, u32[]{:S(2)}) copy-start(bf16[2048,512]{1,0:T(8,128)(2,1)} %param.10) | copy-start | bytes 6291460
  6.5 60.2 %all-gather.7.cloned.1.call-start = ((), (), s32[]{:S(2)}) async-start(), calls=%async_computation.3 | async-start | bytes 2359296 | tf_op jit(solution)/shard_map/all_gather | solution.py:13
  9.9 4.6 %copy-start.13 = (s32[512]{0:T(512)S(1)}, s32[512]{0:T(512)}, u32[]{:S(2)}) copy-start(s32[512]{0:T(512)} %param.13) | copy-start | bytes 6148
  13.4 2.3 %copy-start.4 = (bf16[512,512]{0,1:T(8,128)(2,1)}, bf16[512,512]{0,1:T(8,128)(2,1)S(1)}, u32[]{:S(2)}) copy-start(bf16[512,512]{0,1:T(8,128)(2,1)S(1)} %convolution_convert_fusion) | copy-start | bytes 1572868
  14.5 102.2 %all-gather.5.cloned.1.call-start = ((), (), s32[]{:S(2)}) async-start(), calls=%async_computation.2 | async-start | bytes 2359296 | tf_op jit(solution)/shard_map/all_gather | solution.py:70
  15.7 3.1 %copy-start.9 = (bf16[2048,512]{1,0:T(8,128)(2,1)S(1)}, bf16[2048,512]{1,0:T(8,128)(2,1)}, u32[]{:S(2)}) copy-start(bf16[2048,512]{1,0:T(8,128)(2,1)} %param.11) | copy-start | bytes 6291460
  15.8 3.1 %copy-start.14 = (bf16[512,2048]{1,0:T(8,128)(2,1)S(1)}, bf16[512,2048]{1,0:T(8,128)(2,1)}, u32[]{:S(2)}) copy-start(bf16[512,2048]{1,0:T(8,128)(2,1)} %param.8) | copy-start | bytes 6291460
  18.8 3.8 %copy-start.15 = (u32[32]{0:T(128)S(1)}, u32[32]{0:T(128)}, u32[]{:S(2)}) copy-start(u32[32]{0:T(128)} %constant.64) | copy-start | bytes 388
  20.1 0.8 copy-start.6
  22.0 146.6 %reduce-scatter.2.cloned.1.call-start = ((), (), s32[]{:S(2)}) async-start(), calls=%async_computation.1 | async-start | bytes 5242880 | tf_op jit(solution)/shard_map/reduce_scatter | solution.py:104
  47.1 3.4 %copy-start.5 = (bf16[512,512]{0,1:T(8,128)(2,1)S(1)}, bf16[512,512]{0,1:T(8,128)(2,1)}, u32[]{:S(2)}) copy-start(bf16[512,512]{0,1:T(8,128)(2,1)} %copy-done.4) | copy-start | bytes 1572868
  48.5 3.8 %copy-start.12 = (pred[512,512]{0,1:T(8,128)(4,1)}, pred[512,512]{0,1:T(8,128)(4,1)S(1)}, u32[]{:S(2)}) copy-start(pred[512,512]{0,1:T(8,128)(4,1)S(1)} %fusion.13) | copy-start | bytes 786436
  82.2 1.3 copy-start.3
  82.2 1.7 copy-start.7
  116.7 2.0 %copy-start.2 = (f32[4,128,512]{2,1,0:T(8,128)S(1)}, f32[4,128,512]{2,1,0:T(8,128)}, u32[]{:S(2)}) copy-start(f32[4,128,512]{2,1,0:T(8,128)} %fusion.28) | copy-start | bytes 3145732
  116.7 2.5 %copy-start.8 = (bf16[2048,512]{1,0:T(8,128)(2,1)S(1)}, bf16[2048,512]{1,0:T(8,128)(2,1)}, u32[]{:S(2)}) copy-start(bf16[2048,512]{1,0:T(8,128)(2,1)} %param.9) | copy-start | bytes 6291460
  119.2 2.2 %copy-start.1 = (f32[512,2048]{1,0:T(8,128)S(1)}, f32[512,2048]{1,0:T(8,128)}, u32[]{:S(2)}) copy-start(f32[512,2048]{1,0:T(8,128)} %fusion.31) | copy-start | bytes 12582916
  119.2 2.9 %copy-start.10 = (bf16[2048,512]{1,0:T(8,128)(2,1)S(1)}, bf16[2048,512]{1,0:T(8,128)(2,1)}, u32[]{:S(2)}) copy-start(bf16[2048,512]{1,0:T(8,128)(2,1)} %param.11) | copy-start | bytes 6291460
  119.2 2.9 %copy-start.11 = (bf16[512,4,128]{0,2,1:T(8,128)(2,1)S(1)}, bf16[512,4,128]{0,2,1:T(8,128)(2,1)}, u32[]{:S(2)}) copy-start(bf16[512,4,128]{0,2,1:T(8,128)(2,1)} %fusion.12) | copy-start | bytes 1572868
Sparse Core Ops, SparseCore 0:
  14.6 52.0 all-gather.6
  68.9 47.7 all-gather.4
  125.6 42.9 reduce-scatter.1
where the time goes:
time: 178 us; the launch traced here: 177 us
  waiting for transfers between devices  79.9 us (45%)
  matrix products  30.5 us (17%)
  other arithmetic  23.6 us (13%)
  blocking collectives  23.2 us (13%)
  between operations  13.9 us (8%)
  local copies, waits for them, and re-layouts  5.81 us (3%)
    reduce_scatter x1, waiting for transfers between devices, body(): shares = lax.psum_scatter(total, 'tp', scatter_dimension=0, tiled=True)  43.1 us
    all_gather x1, waiting for transfers between devices, body(): piece = lax.all_gather(carry_out[None], 'ctx', axis=0, tiled=True)  23.6 us
    unnamed x1, blocking collectives  23.2 us
    all_gather x1, waiting for transfers between devices, prefix(): gathered = jax.tree.map(lambda a: lax.all_gather(a, axis), part)  13.1 us
    add x7, other arithmetic, joined(): later[0] + (1.0 - later[1][0]) * earlier[0]  11.2 us
    unnamed x35, local copies, waits for them, and re-layouts  4.35 us
    dot_general x1, matrix products, body(): lax.dot_general(grad_key, w_key, dims, preferred_element_type=jnp.float32)  4.29 us
    sub x7, other arithmetic, joined(): 1.0 - later[1][0]  3.91 us
  transfers between devices with their start and end apart: 3, of which 3 were waited for; matrix products, arithmetic and copies ran while one was open for 22% of the time, Pallas kernels for 0%

commit v1 on v0

--- a/solution.py
+++ b/solution.py
@@ -1,6 +1,10 @@
+import functools
+
 import jax
 import jax.numpy as jnp
 from jax import lax
+from jax.experimental import pallas as pl
+from jax.experimental.pallas import tpu as pltpu
 from jax.sharding import PartitionSpec as P
 
 HD = 128
@@ -105,9 +109,361 @@
     return shares.astype(jnp.bfloat16)
 
 
+NN = ((1,), (0,))
+NT = ((1,), (1,))
+TN = ((0,), (0,))
+COLS = 256
+BF = jnp.bfloat16
+F32 = jnp.float32
+
+
+def dot(a, b, dims):
+    return lax.dot_general(a, b, (dims, ((), ())), preferred_element_type=F32)
+
+
+def fused(
+    nc, nt, tok_hbm, wq_hbm, wk_hbm, wv_hbm, g_hbm, ends_ref, out_ref,
+    tok, w, g, qkv, mask, openc, closec, acc, dcat,
+    st, fl, xfl, xr, cr, co, bs, br, fin,
+    kept, sent, recd, ysent, yrecd,
+    load_sem, fl_sem, x_send, x_recv, c_send, c_recv, b_send, b_recv,
+    rs_send, rs_recv, y_send, y_recv,
+):
+    rows, width = tok.shape
+    heads = g.shape[0]
+    half = heads // 2
+    chunks = width // COLS
+    share = rows // nt
+    ctx = lax.axis_index("ctx")
+    tp = lax.axis_index("tp")
+    par, pair = ctx % 2, ctx // 2
+    pairs = nc // 2
+    lo, hi = tp % 2, tp // 2
+    mate = ctx + 1 - 2 * par
+    core = tp + 1 - 2 * lo
+    over = tp + 2 - 4 * hi
+
+    loads = [
+        pltpu.make_async_copy(tok_hbm, tok, load_sem.at[0]),
+        pltpu.make_async_copy(wk_hbm, w.at[1], load_sem.at[1]),
+        pltpu.make_async_copy(wv_hbm, w.at[2], load_sem.at[2]),
+        pltpu.make_async_copy(wq_hbm, w.at[0], load_sem.at[3]),
+    ]
+    g_loads = [
+        pltpu.make_async_copy(g_hbm.at[:, pl.ds(h * HD, HD)], g.at[h], load_sem.at[4 + h])
+        for h in range(heads)
+    ]
+    for load in loads + g_loads:
+        load.start()
+    barrier = pltpu.get_barrier_semaphore()
+    pl.semaphore_signal(barrier, inc=1, device_id={"ctx": mate}, device_id_type=pl.DeviceIdType.MESH)
+    pl.semaphore_signal(barrier, inc=1, device_id={"tp": core}, device_id_type=pl.DeviceIdType.MESH)
+    pl.semaphore_signal(barrier, inc=1, device_id={"tp": over}, device_id_type=pl.DeviceIdType.MESH)
+
+    @pl.when(pair > 0)
+    def _():
+        pl.semaphore_signal(
+            barrier, inc=1, device_id={"ctx": ctx - 2}, device_id_type=pl.DeviceIdType.MESH
+        )
+
+    @pl.when(pair < pairs - 1)
+    def _():
+        pl.semaphore_signal(
+            barrier, inc=1, device_id={"ctx": ctx + 2}, device_id_type=pl.DeviceIdType.MESH
+        )
+
+    def remote(src, dst, send, recv, device):
+        return pltpu.make_async_remote_copy(
+            src_ref=src, dst_ref=dst, send_sem=send, recv_sem=recv,
+            device_id=device, device_id_type=pl.DeviceIdType.MESH,
+        )
+
+    ends_row = jnp.broadcast_to(ends_ref[...].astype(F32), (HD, rows)).astype(BF)
+    row_id = lax.broadcasted_iota(jnp.int32, (rows, rows), 0)
+    col_id = lax.broadcasted_iota(jnp.int32, (rows, rows), 1)
+    below = (row_id < col_id).astype(F32).astype(BF)
+    above = (col_id < row_id).astype(F32).astype(BF)
+    before_row = dot(ends_row, below, NN)[0:1, :]
+    before_col = dot(above, ends_row, NT)
+    total = jnp.sum(ends_ref[...].astype(F32), axis=1, keepdims=True)
+    openc[...] = (before_col == 0.0).astype(F32)
+    closec[...] = (jnp.broadcast_to(total, (rows, HD)) == before_col).astype(F32)
+    fl[...] = jnp.broadcast_to((total > 0.0).astype(F32), fl.shape)
+    same = before_row == jnp.broadcast_to(before_col[:, 0:1], (rows, rows))
+    mask[...] = jnp.where(same & (col_id <= row_id), 1.0, 0.0)
+
+    waits = 3 + jnp.where(pair > 0, 1, 0) + jnp.where(pair < pairs - 1, 1, 0)
+    pl.semaphore_wait(barrier, waits)
+    flag_copy = remote(fl, xfl, fl_sem.at[0], fl_sem.at[1], {"ctx": mate})
+    flag_copy.start()
+
+    block = min(256, rows)
+    spans = [(at, at + block) for at in range(0, rows, block)]
+
+    def project(which):
+        @pl.loop(0, rows // block)
+        def _(step):
+            at = pl.ds(pl.multiple_of(step * block, block), block)
+            made = dot(tok[at, :], w[which], NN).astype(BF)
+            for h in range(heads):
+                qkv[which, h, at, :] = made[:, h * HD : (h + 1) * HD]
+
+    def x_copy(d, i):
+        return remote(
+            st.at[d, (1 - par) * half + i], xr.at[d, i],
+            x_send.at[d, i], x_recv.at[d, i], {"ctx": mate},
+        )
+
+    loads[0].wait()
+    loads[1].wait()
+    project(1)
+    loads[2].wait()
+    project(2)
+    for i in range(half):
+        h = (1 - par) * half + i
+        st[0, h] = dot((qkv[2, h] * closec[...].astype(BF)), qkv[1, h], TN)
+        x_copy(0, i).start()
+    loads[3].wait()
+    project(0)
+    for load in g_loads:
+        load.wait()
+    for i in range(half):
+        h = (1 - par) * half + i
+        st[1, h] = dot((g[h] * openc[...].astype(BF)), qkv[0, h], TN)
+        x_copy(1, i).start()
+    for i in range(half):
+        h = par * half + i
+        st[0, h] = dot((qkv[2, h] * closec[...].astype(BF)), qkv[1, h], TN)
+        st[1, h] = dot((g[h] * openc[...].astype(BF)), qkv[0, h], TN)
+
+    def within(h):
+        for n, (start, stop) in enumerate(spans):
+            at, upto = slice(start, stop), slice(0, stop)
+            keep = mask[at, upto]
+            scores = (dot(g[h, at, :], qkv[2, h, upto, :], NT) * keep).astype(BF)
+            attn = (dot(qkv[0, h, at, :], qkv[1, h, upto, :], NT) * keep).astype(BF)
+            acc[0, h, at, :] = dot(scores, qkv[1, h, upto, :], NN)
+            dk = dot(scores, qkv[0, h, at, :], TN)
+            dv = dot(attn, g[h, at, :], TN)
+            if n:
+                old = slice(0, start)
+                acc[1, h, old, :] += dk[old]
+                acc[2, h, old, :] += dv[old]
+            acc[1, h, at, :] = dk[at]
+            acc[2, h, at, :] = dv[at]
+
+    def within_some(first, last):
+        @pl.loop(first, last)
+        def _(h):
+            within(h)
+
+    def c_copy(d, i):
+        return remote(
+            co.at[d, i], cr.at[d, i], c_send.at[d, i], c_recv.at[d, i],
+            {"ctx": ctx + 2 - 4 * d},
+        )
+
+    def b_copy(d, i):
+        return remote(bs.at[d, i], br.at[d, i], b_send.at[d, i], b_recv.at[d, i], {"ctx": mate})
+
+    def has_next(d):
+        return ((d == 0) & (pair < pairs - 1)) | ((d == 1) & (pair > 0))
+
+    def has_prev(d):
+        return ((d == 0) & (pair > 0)) | ((d == 1) & (pair < pairs - 1))
+
+    def carry(d):
+        first_here = par == d
+        more, begun = has_next(d), has_prev(d)
+        own_flag, mate_flag = fl[0:1, :], xfl[0:1, :]
+        first_flag = jnp.where(first_here, own_flag, mate_flag)
+        second_flag = jnp.where(first_here, mate_flag, own_flag)
+
+        @pl.when(jnp.logical_not(begun))
+        def _():
+            cr[d] = jnp.zeros(cr.shape[1:], F32)
+
+        for i in range(half):
+            x_copy(d, i).wait_recv()
+            own, other = st[d, par * half + i], xr[d, i]
+            first = jnp.where(first_here, own, other)
+            second = jnp.where(first_here, other, own)
+
+            @pl.when(begun)
+            def _():
+                c_copy(d, i).wait_recv()
+
+            into = cr[d, i]
+            inner = first + (1.0 - first_flag) * into
+
+            @pl.when(more)
+            def _():
+                co[d, i] = second + (1.0 - second_flag) * inner
+                c_copy(d, i).start()
+
+            bs[d, i] = jnp.where(first_here, inner, into)
+            b_copy(d, i).start()
+            fin[d, par * half + i] = jnp.where(first_here, into, inner).astype(BF)
+
+    turn = jnp.where(pair >= pairs // 2, 1, 0)
+    cut = half + half // 2
+    within_some(0, half)
+    flag_copy.wait_recv()
+    carry(turn)
+    within_some(half, cut)
+    carry(1 - turn)
+    within_some(cut, heads)
+
+    scale = 1.0 / HD
+
+    def finish(h):
+        at = pl.ds(pl.multiple_of(h * HD, HD), HD)
+        a_in, b_in = fin[0, h], fin[1, h]
+        opened, closed = openc[...], closec[...]
+        dq = acc[0, h] + opened * dot(g[h], a_in, NN)
+        dk = acc[1, h] + closed * dot(qkv[2, h], b_in, NN)
+        dv = acc[2, h] + closed * dot(qkv[1, h], b_in, NT)
+        dcat[0, :, at] = (scale * dq).astype(BF)
+        dcat[1, :, at] = (scale * dk).astype(BF)
+        dcat[2, :, at] = (scale * dv).astype(BF)
+
+    @pl.loop(0, half)
+    def _(i):
+        finish(par * half + i)
+
+    for i in range(half):
+        for d in range(2):
+            b_copy(d, i).wait_recv()
+            fin[d, (1 - par) * half + i] = br[d, i].astype(BF)
+        finish((1 - par) * half + i)
+
+    def rs_copy(part, j):
+        return remote(
+            sent.at[part, j], recd.at[part, j], rs_send.at[part, j], rs_recv.at[part, j],
+            {"tp": core},
+        )
+
+    def y_copy(j):
+        return remote(ysent.at[j], yrecd.at[j], y_send.at[j], y_recv.at[j], {"tp": over})
+
+    def product(part, j):
+        side = jnp.where(part == 0, 1 - hi, hi)
+        at = pl.ds(pl.multiple_of(side * 2 * share, 2 * share), 2 * share)
+        cols = pl.ds(pl.multiple_of(j * COLS, COLS), COLS)
+        made = dot(dcat[0, at, :], w[0, cols, :], NT)
+        made = made + dot(dcat[1, at, :], w[1, cols, :], NT)
+        made = made + dot(dcat[2, at, :], w[2, cols, :], NT)
+        low, high = made[0:share], made[share : 2 * share]
+        sent[part, j] = jnp.where(lo == 0, high, low)
+        kept[part, j] = jnp.where(lo == 0, low, high)
+        rs_copy(part, j).start()
+
+    def pass_on(j):
+        rs_copy(0, j).wait_recv()
+        ysent[j] = kept[0, j] + recd[0, j]
+        y_copy(j).start()
+
+    product(0, 0)
+
+    @pl.loop(1, chunks)
+    def _(j):
+        product(0, j)
+        pass_on(j - 1)
+
+    product(1, 0)
+    pass_on(chunks - 1)
+
+    @pl.loop(1, chunks)
+    def _(j):
+        product(1, j)
+
+    for j in range(chunks):
+        rs_copy(1, j).wait_recv()
+        y_copy(j).wait_recv()
+        out_ref[:, j * COLS : (j + 1) * COLS] = (kept[1, j] + recd[1, j] + yrecd[j]).astype(BF)
+
+    flag_copy.wait_send()
+    for d in range(2):
+        for i in range(half):
+            x_copy(d, i).wait_send()
+            b_copy(d, i).wait_send()
+
+        @pl.when(has_next(d))
+        def _():
+            for i in range(half):
+                c_copy(d, i).wait_send()
+
+    @pl.loop(0, chunks)
+    def _(j):
+        rs_copy(0, j).wait_send()
+        rs_copy(1, j).wait_send()
+        y_copy(j).wait_send()
+
+
+def fused_body(nc, nt, tokens_in, w_query, w_key, w_value, grad_out, trajectory_ends):
+    rows, width = tokens_in.shape
+    inner = w_query.shape[1]
+    heads = inner // HD
+    half = heads // 2
+    share = rows // nt
+    chunks = width // COLS
+    anywhere = pl.BlockSpec(memory_space=pl.ANY)
+    vmem = pl.BlockSpec(memory_space=pltpu.VMEM)
+    dma = pltpu.SemaphoreType.DMA
+    states = pltpu.VMEM((2, half, HD, HD), F32)
+    piece = (chunks, share, COLS)
+    return pl.pallas_call(
+        functools.partial(fused, nc, nt),
+        out_shape=jax.ShapeDtypeStruct((share, width), BF),
+        in_specs=[anywhere] * 5 + [vmem],
+        out_specs=vmem,
+        scratch_shapes=[
+            pltpu.VMEM((rows, width), BF),
+            pltpu.VMEM((3, width, inner), BF),
+            pltpu.VMEM((heads, rows, HD), BF),
+            pltpu.VMEM((3, heads, rows, HD), BF),
+            pltpu.VMEM((rows, rows), F32),
+            pltpu.VMEM((rows, HD), F32),
+            pltpu.VMEM((rows, HD), F32),
+            pltpu.VMEM((3, heads, rows, HD), F32),
+            pltpu.VMEM((3, rows, inner), BF),
+            pltpu.VMEM((2, heads, HD, HD), F32),
+            pltpu.VMEM((8, HD), F32),
+            pltpu.VMEM((8, HD), F32),
+            states, states, states, states, states,
+            pltpu.VMEM((2, heads, HD, HD), BF),
+            pltpu.VMEM((2, *piece), F32),
+            pltpu.VMEM((2, *piece), F32),
+            pltpu.VMEM((2, *piece), F32),
+            pltpu.VMEM(piece, F32),
+            pltpu.VMEM(piece, F32),
+            dma((4 + heads,)),
+            dma((2,)),
+            dma((2, half)), dma((2, half)),
+            dma((2, half)), dma((2, half)),
+            dma((2, half)), dma((2, half)),
+            dma((2, chunks)), dma((2, chunks)),
+            dma((chunks,)), dma((chunks,)),
+        ],
+        compiler_params=pltpu.CompilerParams(
+            collective_id=0, has_side_effects=True, vmem_limit_bytes=48 * 2**20
+        ),
+    )(tokens_in, w_query, w_key, w_value, grad_out, trajectory_ends.reshape(1, rows))
+
+
 def solution(mesh):
+    nc, nt = mesh.shape["ctx"], mesh.shape["tp"]
+
+    def local(tokens_in, w_query, w_key, w_value, grad_out, trajectory_ends):
+        rows, width = tokens_in.shape
+        heads = w_query.shape[1] // HD
+        fits = nt == 4 and nc % 2 == 0 and heads % 2 == 0 and rows <= 512
+        fits = fits and width % COLS == 0 and rows % 256 == 0
+        call = functools.partial(fused_body, nc, nt) if fits else body
+        return call(tokens_in, w_query, w_key, w_value, grad_out, trajectory_ends)
+
     return jax.shard_map(
-        body,
+        local,
         mesh=mesh,
         in_specs=(
             P("ctx", None),

time: 178 us -> 61.5 us (0.35)
  waiting for transfers between devices: 79.9 us -> 0 us
  Pallas kernels: 0 us -> 55.6 us
  matrix products: 30.5 us -> 0 us
  other arithmetic: 23.6 us -> 0 us
  blocking collectives: 23.2 us -> 0 us
  between operations: 13.9 us -> 0.01 us
    pallas_call x0 -> x1, Pallas kernels: none -> 55.6 us  [fused_body(): pl.pallas_call(functools.partial(fused, nc, nt), out_shape=jax.ShapeDtype...]
    reduce_scatter x1 -> x0, waiting for transfers between devices: 43.1 us -> none  [body(): shares = lax.psum_scatter(total, 'tp', scatter_dimension=0, tiled=True)]
    all_gather x2 -> x0, waiting for transfers between devices: 36.7 us -> none  [the longest x1 23.6 us: body(): piece = lax.all_gather(carry_out[None], 'ctx', axis=0, tiled=True)]
    dot_general x15 -> x0, matrix products: 30.5 us -> none  [the longest x1 4.29 us: body(): lax.dot_general(grad_key, w_key, dims, preferred_element_type=jnp.float32)]
    unnamed x1 -> x0, blocking collectives: 23.2 us -> none
    add x7 -> x0, other arithmetic: 11.2 us -> none  [joined(): later[0] + (1.0 - later[1][0]) * earlier[0]]
    convert_element_type x6 -> x0, other arithmetic: 3.95 us -> none  [the longest x1 2.08 us: body(): return shares.astype(jnp.bfloat16)]
    sub x7 -> x0, other arithmetic: 3.91 us -> none  [joined(): 1.0 - later[1][0]]
  transfers between devices with their start and end apart: 3 -> 0, of which waited for: 3 -> 0; matrix products, arithmetic and copies ran while one was open for 22% -> 0% of each run, Pallas kernels for 0% -> 0%
where the time goes in v1:
time: 61.5 us; the launch traced here: 61.3 us
  Pallas kernels  55.6 us (90%)
  local copies, waits for them, and re-layouts  5.7 us (9%)
    pallas_call x1, Pallas kernels, fused_body(): pl.pallas_call(functools.partial(fused, nc, nt), out_shape=jax.ShapeDtype...  55.6 us
    unnamed x9, local copies, waits for them, and re-layouts  5.7 us

profile of v1, /device:TPU:0, one launch (start us, length us, event | category | flops | bytes accessed | tf_op | source)
XLA Modules:
  0.0 61.3 jit_solution(16771517746834025336)
XLA Ops:
  0.0 0.0 copy-start
  0.0 1.6 %copy-done = bf16[512,2048]{1,0:T(8,128)(2,1)S(1)} copy-done((bf16[512,2048]{1,0:T(8,128)(2,1)S(1)}, bf16[512,2048]{1,0:T(8,128)(2,1)}, u32[]{:S(2)}) %copy-start) | copy-done | bytes 2097176
  1.6 0.0 copy-start.1
  1.6 1.6 %copy-done.1 = bf16[2048,512]{1,0:T(8,128)(2,1)S(1)} copy-done((bf16[2048,512]{1,0:T(8,128)(2,1)S(1)}, bf16[2048,512]{1,0:T(8,128)(2,1)}, u32[]{:S(2)}) %copy-start.1) | copy-done | bytes 2097176
  3.2 0.0 copy-start.2
  3.2 1.0 %copy-done.2 = bf16[512,512]{1,0:T(8,128)(2,1)S(1)} copy-done((bf16[512,512]{1,0:T(8,128)(2,1)S(1)}, bf16[512,512]{1,0:T(8,128)(2,1)}, u32[]{:S(2)}) %copy-start.2) | copy-done | bytes 524312
  4.2 0.0 copy-start.3
  4.2 0.7 %copy-done.3 = s32[512]{0:T(512)S(1)} copy-done((s32[512]{0:T(512)S(1)}, s32[512]{0:T(512)}, u32[]{:S(2)}) %copy-start.3) | copy-done | bytes 2072
  4.9 55.6 %shard_map.64 = bf16[128,2048]{1,0:T(8,128)(2,1)S(1)} custom-call(bf16[512,2048]{1,0:T(8,128)(2,1)S(1)} %copy-done, bf16[2048,512]{1,0:T(8,128)(2,1)S(1)} %copy-done.1, bf16[2048,512]{1,0:T(8,128)(2,1)} %wk_hbm.1, bf16[2048,512]{1,0:T(8,128)(2,1)} %wv_hbm.1, bf16[512,512]{1,0:T(8,128)(2,1)S(1)} %copy-done.2, s32[1,512]{1,0:T(1,128)S(1)} %bitcast.1), custom_call_target="tpu_custom_call" | custom-call | tf_op jit(solution)/shard_map/pallas_call | solution.py:415
  60.5 0.8 %copy.8 = bf16[128,2048]{1,0:T(8,128)(2,1)} copy(bf16[128,2048]{1,0:T(8,128)(2,1)S(1)} %shard_map.64) | data formatting | bytes 1048576
Async XLA Ops:
  0.0 1.6 %copy-start = (bf16[512,2048]{1,0:T(8,128)(2,1)S(1)}, bf16[512,2048]{1,0:T(8,128)(2,1)}, u32[]{:S(2)}) copy-start(bf16[512,2048]{1,0:T(8,128)(2,1)} %tok_hbm.1) | copy-start | bytes 6291460
  1.6 1.6 %copy-start.1 = (bf16[2048,512]{1,0:T(8,128)(2,1)S(1)}, bf16[2048,512]{1,0:T(8,128)(2,1)}, u32[]{:S(2)}) copy-start(bf16[2048,512]{1,0:T(8,128)(2,1)} %wq_hbm.1) | copy-start | bytes 6291460
  3.2 1.0 %copy-start.2 = (bf16[512,512]{1,0:T(8,128)(2,1)S(1)}, bf16[512,512]{1,0:T(8,128)(2,1)}, u32[]{:S(2)}) copy-start(bf16[512,512]{1,0:T(8,128)(2,1)} %g_hbm.1) | copy-start | bytes 1572868
  4.2 0.7 %copy-start.3 = (s32[512]{0:T(512)S(1)}, s32[512]{0:T(512)}, u32[]{:S(2)}) copy-start(s32[512]{0:T(512)} %param.11) | copy-start | bytes 6148

commit v2 on v1

--- a/solution.py
+++ b/solution.py
@@ -113,6 +113,7 @@
 NT = ((1,), (1,))
 TN = ((0,), (0,))
 COLS = 256
+SPLIT = 2
 BF = jnp.bfloat16
 F32 = jnp.float32
 
@@ -132,6 +133,8 @@
     rows, width = tok.shape
     heads = g.shape[0]
     half = heads // 2
+    pieces = half * SPLIT
+    deep = HD // SPLIT
     chunks = width // COLS
     share = rows // nt
     ctx = lax.axis_index("ctx")
@@ -143,18 +146,33 @@
     core = tp + 1 - 2 * lo
     over = tp + 2 - 4 * hi
 
-    loads = [
-        pltpu.make_async_copy(tok_hbm, tok, load_sem.at[0]),
-        pltpu.make_async_copy(wk_hbm, w.at[1], load_sem.at[1]),
-        pltpu.make_async_copy(wv_hbm, w.at[2], load_sem.at[2]),
-        pltpu.make_async_copy(wq_hbm, w.at[0], load_sem.at[3]),
+    turn = jnp.where(pair >= pairs // 2, 1, 0)
+    token_load = pltpu.make_async_copy(tok_hbm, tok, load_sem.at[0])
+    weight_loads = [
+        pltpu.make_async_copy(ref, w.at[n], load_sem.at[1 + n])
+        for n, ref in enumerate((wq_hbm, wk_hbm, wv_hbm))
     ]
     g_loads = [
         pltpu.make_async_copy(g_hbm.at[:, pl.ds(h * HD, HD)], g.at[h], load_sem.at[4 + h])
         for h in range(heads)
     ]
-    for load in loads + g_loads:
-        load.start()
+    token_load.start()
+
+    @pl.when(turn == 0)
+    def _():
+        for n in (1, 2, 0):
+            weight_loads[n].start()
+        for load in g_loads:
+            load.start()
+
+    @pl.when(turn == 1)
+    def _():
+        weight_loads[0].start()
+        for load in g_loads:
+            load.start()
+        for n in (1, 2):
+            weight_loads[n].start()
+
     barrier = pltpu.get_barrier_semaphore()
     pl.semaphore_signal(barrier, inc=1, device_id={"ctx": mate}, device_id_type=pl.DeviceIdType.MESH)
     pl.semaphore_signal(barrier, inc=1, device_id={"tp": core}, device_id_type=pl.DeviceIdType.MESH)
@@ -210,31 +228,52 @@
 
     def x_copy(d, i):
         return remote(
-            st.at[d, (1 - par) * half + i], xr.at[d, i],
+            st.at[d, (1 - par) * pieces + i], xr.at[d, i],
             x_send.at[d, i], x_recv.at[d, i], {"ctx": mate},
         )
 
-    loads[0].wait()
-    loads[1].wait()
-    project(1)
-    loads[2].wait()
-    project(2)
+    def state(d, h):
+        if d == 0:
+            made = dot(qkv[2, h] * closec[...].astype(BF), qkv[1, h], TN)
+        else:
+            made = dot(g[h] * openc[...].astype(BF), qkv[0, h], TN)
+        for n in range(SPLIT):
+            st[d, h * SPLIT + n] = made[n * deep : (n + 1) * deep]
+
+    def give(d):
+        for i in range(half):
+            state(d, (1 - par) * half + i)
+            for n in range(SPLIT):
+                x_copy(d, i * SPLIT + n).start()
+
+    def forward_part():
+        for n in (1, 2):
+            weight_loads[n].wait()
+            project(n)
+        give(0)
+
+    def backward_part():
+        weight_loads[0].wait()
+        project(0)
+        for load in g_loads:
+            load.wait()
+        give(1)
+
+    token_load.wait()
+
+    @pl.when(turn == 0)
+    def _():
+        forward_part()
+        backward_part()
+
+    @pl.when(turn == 1)
+    def _():
+        backward_part()
+        forward_part()
+
     for i in range(half):
-        h = (1 - par) * half + i
-        st[0, h] = dot((qkv[2, h] * closec[...].astype(BF)), qkv[1, h], TN)
-        x_copy(0, i).start()
-    loads[3].wait()
-    project(0)
-    for load in g_loads:
-        load.wait()
-    for i in range(half):
-        h = (1 - par) * half + i
-        st[1, h] = dot((g[h] * openc[...].astype(BF)), qkv[0, h], TN)
-        x_copy(1, i).start()
-    for i in range(half):
-        h = par * half + i
-        st[0, h] = dot((qkv[2, h] * closec[...].astype(BF)), qkv[1, h], TN)
-        st[1, h] = dot((g[h] * openc[...].astype(BF)), qkv[0, h], TN)
+        state(0, par * half + i)
+        state(1, par * half + i)
 
     def within(h):
         for n, (start, stop) in enumerate(spans):
@@ -272,6 +311,9 @@
     def has_prev(d):
         return ((d == 0) & (pair > 0)) | ((d == 1) & (pair < pairs - 1))
 
+    def place(i):
+        return slice(i % SPLIT * deep, (i % SPLIT + 1) * deep)
+
     def carry(d):
         first_here = par == d
         more, begun = has_next(d), has_prev(d)
@@ -283,9 +325,9 @@
         def _():
             cr[d] = jnp.zeros(cr.shape[1:], F32)
 
-        for i in range(half):
+        for i in range(pieces):
             x_copy(d, i).wait_recv()
-            own, other = st[d, par * half + i], xr[d, i]
+            own, other = st[d, par * pieces + i], xr[d, i]
             first = jnp.where(first_here, own, other)
             second = jnp.where(first_here, other, own)
 
@@ -303,9 +345,9 @@
 
             bs[d, i] = jnp.where(first_here, inner, into)
             b_copy(d, i).start()
-            fin[d, par * half + i] = jnp.where(first_here, into, inner).astype(BF)
-
-    turn = jnp.where(pair >= pairs // 2, 1, 0)
+            mine = jnp.where(first_here, into, inner).astype(BF)
+            fin[d, par * half + i // SPLIT, place(i), :] = mine
+
     cut = half + half // 2
     within_some(0, half)
     flag_copy.wait_recv()
@@ -316,26 +358,33 @@
 
     scale = 1.0 / HD
 
-    def finish(h):
+    def finish(d, h):
         at = pl.ds(pl.multiple_of(h * HD, HD), HD)
-        a_in, b_in = fin[0, h], fin[1, h]
-        opened, closed = openc[...], closec[...]
-        dq = acc[0, h] + opened * dot(g[h], a_in, NN)
-        dk = acc[1, h] + closed * dot(qkv[2, h], b_in, NN)
-        dv = acc[2, h] + closed * dot(qkv[1, h], b_in, NT)
-        dcat[0, :, at] = (scale * dq).astype(BF)
-        dcat[1, :, at] = (scale * dk).astype(BF)
-        dcat[2, :, at] = (scale * dv).astype(BF)
-
-    @pl.loop(0, half)
-    def _(i):
-        finish(par * half + i)
-
-    for i in range(half):
-        for d in range(2):
-            b_copy(d, i).wait_recv()
-            fin[d, (1 - par) * half + i] = br[d, i].astype(BF)
-        finish((1 - par) * half + i)
+
+        @pl.when(d == 0)
+        def _():
+            dq = acc[0, h] + openc[...] * dot(g[h], fin[0, h], NN)
+            dcat[0, :, at] = (scale * dq).astype(BF)
+
+        @pl.when(d == 1)
+        def _():
+            b_in, closed = fin[1, h], closec[...]
+            dk = acc[1, h] + closed * dot(qkv[2, h], b_in, NN)
+            dv = acc[2, h] + closed * dot(qkv[1, h], b_in, NT)
+            dcat[1, :, at] = (scale * dk).astype(BF)
+            dcat[2, :, at] = (scale * dv).astype(BF)
+
+    @pl.loop(0, 2 * half)
+    def _(n):
+        finish((n // half + turn) % 2, par * half + n % half)
+
+    for d in (turn, 1 - turn):
+        for i in range(half):
+            h = (1 - par) * half + i
+            for n in range(i * SPLIT, (i + 1) * SPLIT):
+                b_copy(d, n).wait_recv()
+                fin[d, h, place(n), :] = br[d, n].astype(BF)
+            finish(d, h)
 
     def rs_copy(part, j):
         return remote(
@@ -384,13 +433,13 @@
 
     flag_copy.wait_send()
     for d in range(2):
-        for i in range(half):
+        for i in range(pieces):
             x_copy(d, i).wait_send()
             b_copy(d, i).wait_send()
 
         @pl.when(has_next(d))
         def _():
-            for i in range(half):
+            for i in range(pieces):
                 c_copy(d, i).wait_send()
 
     @pl.loop(0, chunks)
@@ -410,7 +459,9 @@
     anywhere = pl.BlockSpec(memory_space=pl.ANY)
     vmem = pl.BlockSpec(memory_space=pltpu.VMEM)
     dma = pltpu.SemaphoreType.DMA
-    states = pltpu.VMEM((2, half, HD, HD), F32)
+    pieces = half * SPLIT
+    deep = HD // SPLIT
+    states = pltpu.VMEM((2, pieces, deep, HD), F32)
     piece = (chunks, share, COLS)
     return pl.pallas_call(
         functools.partial(fused, nc, nt),
@@ -427,7 +478,7 @@
             pltpu.VMEM((rows, HD), F32),
             pltpu.VMEM((3, heads, rows, HD), F32),
             pltpu.VMEM((3, rows, inner), BF),
-            pltpu.VMEM((2, heads, HD, HD), F32),
+            pltpu.VMEM((2, heads * SPLIT, deep, HD), F32),
             pltpu.VMEM((8, HD), F32),
             pltpu.VMEM((8, HD), F32),
             states, states, states, states, states,
@@ -439,14 +490,14 @@
             pltpu.VMEM(piece, F32),
             dma((4 + heads,)),
             dma((2,)),
-            dma((2, half)), dma((2, half)),
-            dma((2, half)), dma((2, half)),
-            dma((2, half)), dma((2, half)),
+            dma((2, pieces)), dma((2, pieces)),
+            dma((2, pieces)), dma((2, pieces)),
+            dma((2, pieces)), dma((2, pieces)),
             dma((2, chunks)), dma((2, chunks)),
             dma((chunks,)), dma((chunks,)),
         ],
         compiler_params=pltpu.CompilerParams(
-            collective_id=0, has_side_effects=True, vmem_limit_bytes=48 * 2**20
+            collective_id=0, has_side_effects=True, vmem_limit_bytes=60 * 2**20
         ),
     )(tokens_in, w_query, w_key, w_value, grad_out, trajectory_ends.reshape(1, rows))
 

time: 61.5 us -> 57.3 us (0.932)
  local copies, waits for them, and re-layouts: 5.7 us -> 1.88 us
    unnamed x9 -> x1, local copies, waits for them, and re-layouts: 5.7 us -> 1.88 us
where the time goes in v2:
time: 57.3 us; the launch traced here: 57.1 us
  Pallas kernels  55.2 us (96%)
  local copies, waits for them, and re-layouts  1.88 us (3%)
    pallas_call x1, Pallas kernels, fused_body(): pl.pallas_call(functools.partial(fused, nc, nt), out_shape=jax.ShapeDtype...  55.2 us
    unnamed x1, local copies, waits for them, and re-layouts  1.88 us

profile of v2, /device:TPU:0, one launch (start us, length us, event | category | flops | bytes accessed | tf_op | source)
XLA Modules:
  0.0 57.1 jit_solution(3851937158779011861)
XLA Ops:
  0.0 55.2 %shard_map.64 = bf16[128,2048]{1,0:T(8,128)(2,1)} custom-call(bf16[512,2048]{1,0:T(8,128)(2,1)} %tok_hbm.1, bf16[2048,512]{1,0:T(8,128)(2,1)} %wq_hbm.1, bf16[2048,512]{1,0:T(8,128)(2,1)} %wk_hbm.1, bf16[2048,512]{1,0:T(8,128)(2,1)} %wv_hbm.1, bf16[512,512]{1,0:T(8,128)(2,1)} %g_hbm.1, s32[1,512]{1,0:T(1,128)} %bitcast.1), custom_call_target="tpu_custom_call" | custom-call | tf_op jit(solution)/shard_map/pallas_call | solution.py:466
  55.3 1.9 %copy.8 = bf16[128,2048]{1,0:T(8,128)(2,1)} copy(bf16[128,2048]{1,0:T(8,128)(2,1)} %shard_map.64) | data formatting | bytes 1048576

commit v3 on v2

--- a/solution.py
+++ b/solution.py
@@ -123,8 +123,8 @@
 
 
 def fused(
-    nc, nt, tok_hbm, wq_hbm, wk_hbm, wv_hbm, g_hbm, ends_ref, out_ref,
-    tok, w, g, qkv, mask, openc, closec, acc, dcat,
+    nc, nt, tok_hbm, wq_hbm, wk_hbm, wv_hbm, g_hbm, ends_hbm, out_ref,
+    ends_ref, tok, w, g, qkv, mask, flip, openc, closec, acc, dcat,
     st, fl, xfl, xr, cr, co, bs, br, fin,
     kept, sent, recd, ysent, yrecd,
     load_sem, fl_sem, x_send, x_recv, c_send, c_recv, b_send, b_recv,
@@ -156,6 +156,8 @@
         pltpu.make_async_copy(g_hbm.at[:, pl.ds(h * HD, HD)], g.at[h], load_sem.at[4 + h])
         for h in range(heads)
     ]
+    ends_load = pltpu.make_async_copy(ends_hbm, ends_ref, load_sem.at[4 + heads])
+    ends_load.start()
     token_load.start()
 
     @pl.when(turn == 0)
@@ -196,6 +198,7 @@
             device_id=device, device_id_type=pl.DeviceIdType.MESH,
         )
 
+    ends_load.wait()
     ends_row = jnp.broadcast_to(ends_ref[...].astype(F32), (HD, rows)).astype(BF)
     row_id = lax.broadcasted_iota(jnp.int32, (rows, rows), 0)
     col_id = lax.broadcasted_iota(jnp.int32, (rows, rows), 1)
@@ -208,12 +211,8 @@
     closec[...] = (jnp.broadcast_to(total, (rows, HD)) == before_col).astype(F32)
     fl[...] = jnp.broadcast_to((total > 0.0).astype(F32), fl.shape)
     same = before_row == jnp.broadcast_to(before_col[:, 0:1], (rows, rows))
-    mask[...] = jnp.where(same & (col_id <= row_id), 1.0, 0.0)
-
-    waits = 3 + jnp.where(pair > 0, 1, 0) + jnp.where(pair < pairs - 1, 1, 0)
-    pl.semaphore_wait(barrier, waits)
-    flag_copy = remote(fl, xfl, fl_sem.at[0], fl_sem.at[1], {"ctx": mate})
-    flag_copy.start()
+    mask[...] = (same & (col_id <= row_id)).astype(F32).astype(BF)
+    flip[...] = (same & (row_id <= col_id)).astype(F32).astype(BF)
 
     block = min(256, rows)
     spans = [(at, at + block) for at in range(0, rows, block)]
@@ -246,50 +245,57 @@
             for n in range(SPLIT):
                 x_copy(d, i * SPLIT + n).start()
 
-    def forward_part():
+    def keys_values():
         for n in (1, 2):
             weight_loads[n].wait()
             project(n)
-        give(0)
-
-    def backward_part():
+
+    def queries():
         weight_loads[0].wait()
         project(0)
-        for load in g_loads:
-            load.wait()
+
+    token_load.wait()
+
+    @pl.when(turn == 0)
+    def _():
+        keys_values()
+
+    @pl.when(turn == 1)
+    def _():
+        queries()
+
+    for load in g_loads:
+        load.wait()
+    waits = 3 + jnp.where(pair > 0, 1, 0) + jnp.where(pair < pairs - 1, 1, 0)
+    pl.semaphore_wait(barrier, waits)
+    flag_copy = remote(fl, xfl, fl_sem.at[0], fl_sem.at[1], {"ctx": mate})
+    flag_copy.start()
+
+    @pl.when(turn == 0)
+    def _():
+        give(0)
+        queries()
         give(1)
 
-    token_load.wait()
-
-    @pl.when(turn == 0)
-    def _():
-        forward_part()
-        backward_part()
-
     @pl.when(turn == 1)
     def _():
-        backward_part()
-        forward_part()
+        give(1)
+        keys_values()
+        give(0)
 
     for i in range(half):
         state(0, par * half + i)
         state(1, par * half + i)
 
     def within(h):
-        for n, (start, stop) in enumerate(spans):
-            at, upto = slice(start, stop), slice(0, stop)
-            keep = mask[at, upto]
-            scores = (dot(g[h, at, :], qkv[2, h, upto, :], NT) * keep).astype(BF)
-            attn = (dot(qkv[0, h, at, :], qkv[1, h, upto, :], NT) * keep).astype(BF)
+        for start, stop in spans:
+            at, upto, onward = slice(start, stop), slice(0, stop), slice(start, rows)
+            scores = dot(g[h, at, :], qkv[2, h, upto, :], NT).astype(BF) * mask[at, upto]
             acc[0, h, at, :] = dot(scores, qkv[1, h, upto, :], NN)
-            dk = dot(scores, qkv[0, h, at, :], TN)
-            dv = dot(attn, g[h, at, :], TN)
-            if n:
-                old = slice(0, start)
-                acc[1, h, old, :] += dk[old]
-                acc[2, h, old, :] += dv[old]
-            acc[1, h, at, :] = dk[at]
-            acc[2, h, at, :] = dv[at]
+            turned = dot(qkv[2, h, at, :], g[h, onward, :], NT).astype(BF) * flip[at, onward]
+            acc[1, h, at, :] = dot(turned, qkv[0, h, onward, :], NN)
+            attn = dot(qkv[1, h, at, :], qkv[0, h, onward, :], NT).astype(BF) * flip[at, onward]
+            acc[2, h, at, :] = dot(attn, g[h, onward, :], NN)
 
     def within_some(first, last):
         @pl.loop(first, last)
@@ -348,13 +354,15 @@
             mine = jnp.where(first_here, into, inner).astype(BF)
             fin[d, par * half + i // SPLIT, place(i), :] = mine
 
-    cut = half + half // 2
-    within_some(0, half)
+    at_end = (pair == 0) | (pair == pairs - 1)
+    early = jnp.where(at_end, 0, heads // 4)
+    late = jnp.where(at_end, heads - heads // 4, heads // 2)
     flag_copy.wait_recv()
+    within_some(0, early)
     carry(turn)
-    within_some(half, cut)
+    within_some(early, late)
     carry(1 - turn)
-    within_some(cut, heads)
+    within_some(late, heads)
 
     scale = 1.0 / HD
 
@@ -456,24 +464,27 @@
     half = heads // 2
     share = rows // nt
     chunks = width // COLS
-    anywhere = pl.BlockSpec(memory_space=pl.ANY)
+    outside = pl.BlockSpec(memory_space=pltpu.HBM)
     vmem = pl.BlockSpec(memory_space=pltpu.VMEM)
     dma = pltpu.SemaphoreType.DMA
     pieces = half * SPLIT
     deep = HD // SPLIT
     states = pltpu.VMEM((2, pieces, deep, HD), F32)
     piece = (chunks, share, COLS)
+    operands = (tokens_in, w_query, w_key, w_value, grad_out, trajectory_ends.reshape(1, rows))
     return pl.pallas_call(
         functools.partial(fused, nc, nt),
         out_shape=jax.ShapeDtypeStruct((share, width), BF),
-        in_specs=[anywhere] * 5 + [vmem],
+        in_specs=[outside] * 6,
         out_specs=vmem,
         scratch_shapes=[
+            pltpu.VMEM((1, rows), jnp.int32),
             pltpu.VMEM((rows, width), BF),
             pltpu.VMEM((3, width, inner), BF),
             pltpu.VMEM((heads, rows, HD), BF),
             pltpu.VMEM((3, heads, rows, HD), BF),
-            pltpu.VMEM((rows, rows), F32),
+            pltpu.VMEM((rows, rows), BF),
+            pltpu.VMEM((rows, rows), BF),
             pltpu.VMEM((rows, HD), F32),
             pltpu.VMEM((rows, HD), F32),
             pltpu.VMEM((3, heads, rows, HD), F32),
@@ -488,7 +499,7 @@
             pltpu.VMEM((2, *piece), F32),
             pltpu.VMEM(piece, F32),
             pltpu.VMEM(piece, F32),
-            dma((4 + heads,)),
+            dma((5 + heads,)),
             dma((2,)),
             dma((2, pieces)), dma((2, pieces)),
             dma((2, pieces)), dma((2, pieces)),
@@ -497,9 +508,9 @@
             dma((chunks,)), dma((chunks,)),
         ],
         compiler_params=pltpu.CompilerParams(
-            collective_id=0, has_side_effects=True, vmem_limit_bytes=60 * 2**20
+            collective_id=0, has_side_effects=True, vmem_limit_bytes=48 * 2**20
         ),
-    )(tokens_in, w_query, w_key, w_value, grad_out, trajectory_ends.reshape(1, rows))
+    )(*[pltpu.with_memory_space_constraint(x, pltpu.HBM) for x in operands])
 
 
 def solution(mesh):

time: 57.3 us -> 53.1 us (0.927)
  Pallas kernels: 55.2 us -> 52.1 us
  local copies, waits for them, and re-layouts: 1.88 us -> 0.8 us
    pallas_call x1, Pallas kernels: 55.2 us -> 52.1 us  [fused_body(): pl.pallas_call(functools.partial(fused, nc, nt), out_shape=jax.ShapeDtype...]
    unnamed x1, local copies, waits for them, and re-layouts: 1.88 us -> 0.8 us
where the time goes in v3:
time: 53.1 us; the launch traced here: 52.9 us
  Pallas kernels  52.1 us (98%)
  local copies, waits for them, and re-layouts  0.8 us (2%)
    pallas_call x1, Pallas kernels, fused_body(): pl.pallas_call(functools.partial(fused, nc, nt), out_shape=jax.ShapeDtype...  52.1 us

profile of v3, /device:TPU:0, one launch (start us, length us, event | category | flops | bytes accessed | tf_op | source)
XLA Modules:
  0.0 52.9 jit_solution(11747702954259442949)
XLA Ops:
  0.0 52.1 %shard_map.64 = bf16[128,2048]{1,0:T(8,128)(2,1)S(1)} custom-call(bf16[512,2048]{1,0:T(8,128)(2,1)} %tok_hbm.1, bf16[2048,512]{1,0:T(8,128)(2,1)} %wq_hbm.1, bf16[2048,512]{1,0:T(8,128)(2,1)} %wk_hbm.1, bf16[2048,512]{1,0:T(8,128)(2,1)} %wv_hbm.1, bf16[512,512]{1,0:T(8,128)(2,1)} %g_hbm.1, s32[1,512]{1,0:T(1,128)} %bitcast.1), custom_call_target="tpu_custom_call" | custom-call | tf_op jit(solution)/shard_map/pallas_call | solution.py:475
  52.1 0.8 %copy.8 = bf16[128,2048]{1,0:T(8,128)(2,1)} copy(bf16[128,2048]{1,0:T(8,128)(2,1)S(1)} %shard_map.64) | data formatting | bytes 1048576

commit v4 on v3

--- a/solution.py
+++ b/solution.py
@@ -124,7 +124,7 @@
 
 def fused(
     nc, nt, tok_hbm, wq_hbm, wk_hbm, wv_hbm, g_hbm, ends_hbm, out_ref,
-    ends_ref, tok, w, g, qkv, mask, flip, openc, closec, acc, dcat,
+    ends_ref, tok, w, g, qkv, mask, flip, count, openc, closec, acc, dcat,
     st, fl, xfl, xr, cr, co, bs, br, fin,
     kept, sent, recd, ysent, yrecd,
     load_sem, fl_sem, x_send, x_recv, c_send, c_recv, b_send, b_recv,
@@ -132,6 +132,7 @@
 ):
     rows, width = tok.shape
     heads = g.shape[0]
+    inner = w.shape[2]
     half = heads // 2
     pieces = half * SPLIT
     deep = HD // SPLIT
@@ -147,33 +148,46 @@
     over = tp + 2 - 4 * hi
 
     turn = jnp.where(pair >= pairs // 2, 1, 0)
-    token_load = pltpu.make_async_copy(tok_hbm, tok, load_sem.at[0])
-    weight_loads = [
-        pltpu.make_async_copy(ref, w.at[n], load_sem.at[1 + n])
-        for n, ref in enumerate((wq_hbm, wk_hbm, wv_hbm))
+    block = rows // 2
+    token_loads = [
+        pltpu.make_async_copy(tok_hbm.at[at, :], tok.at[at, :], load_sem.at[n])
+        for n, at in enumerate((slice(0, block), slice(block, rows)))
     ]
+    sides = inner // COLS
+
+    def weight_load(ref, which, side):
+        at = pl.ds(pl.multiple_of(side * COLS, COLS), COLS)
+        return pltpu.make_async_copy(
+            ref.at[:, at], w.at[which, :, at], load_sem.at[3 + heads + which * sides + side]
+        )
+
+    def start_weight(ref, which):
+        for side in range(sides):
+            weight_load(ref, which, side).start()
+
     g_loads = [
-        pltpu.make_async_copy(g_hbm.at[:, pl.ds(h * HD, HD)], g.at[h], load_sem.at[4 + h])
+        pltpu.make_async_copy(g_hbm.at[:, pl.ds(h * HD, HD)], g.at[h], load_sem.at[2 + h])
         for h in range(heads)
     ]
-    ends_load = pltpu.make_async_copy(ends_hbm, ends_ref, load_sem.at[4 + heads])
+    ends_load = pltpu.make_async_copy(ends_hbm, ends_ref, load_sem.at[2 + heads])
     ends_load.start()
-    token_load.start()
+    for load in token_loads:
+        load.start()
+
+    @pl.when(turn == 1)
+    def _():
+        start_weight(wq_hbm, 0)
+        for load in g_loads:
+            load.start()
+
+    start_weight(wk_hbm, 1)
+    start_weight(wv_hbm, 2)
 
     @pl.when(turn == 0)
     def _():
-        for n in (1, 2, 0):
-            weight_loads[n].start()
+        start_weight(wq_hbm, 0)
         for load in g_loads:
             load.start()
-
-    @pl.when(turn == 1)
-    def _():
-        weight_loads[0].start()
-        for load in g_loads:
-            load.start()
-        for n in (1, 2):
-            weight_loads[n].start()
 
     barrier = pltpu.get_barrier_semaphore()
     pl.semaphore_signal(barrier, inc=1, device_id={"ctx": mate}, device_id_type=pl.DeviceIdType.MESH)
@@ -202,28 +216,23 @@
     ends_row = jnp.broadcast_to(ends_ref[...].astype(F32), (HD, rows)).astype(BF)
     row_id = lax.broadcasted_iota(jnp.int32, (rows, rows), 0)
     col_id = lax.broadcasted_iota(jnp.int32, (rows, rows), 1)
-    below = (row_id < col_id).astype(F32).astype(BF)
     above = (col_id < row_id).astype(F32).astype(BF)
-    before_row = dot(ends_row, below, NN)[0:1, :]
     before_col = dot(above, ends_row, NT)
     total = jnp.sum(ends_ref[...].astype(F32), axis=1, keepdims=True)
+    count[...] = before_col
     openc[...] = (before_col == 0.0).astype(F32)
     closec[...] = (jnp.broadcast_to(total, (rows, HD)) == before_col).astype(F32)
     fl[...] = jnp.broadcast_to((total > 0.0).astype(F32), fl.shape)
-    same = before_row == jnp.broadcast_to(before_col[:, 0:1], (rows, rows))
-    mask[...] = (same & (col_id <= row_id)).astype(F32).astype(BF)
-    flip[...] = (same & (row_id <= col_id)).astype(F32).astype(BF)
-
-    block = min(256, rows)
-    spans = [(at, at + block) for at in range(0, rows, block)]
-
-    def project(which):
-        @pl.loop(0, rows // block)
-        def _(step):
-            at = pl.ds(pl.multiple_of(step * block, block), block)
-            made = dot(tok[at, :], w[which], NN).astype(BF)
-            for h in range(heads):
-                qkv[which, h, at, :] = made[:, h * HD : (h + 1) * HD]
+
+    spans = [(0, block), (block, rows)]
+    per_side = COLS // HD
+
+    def project(which, side):
+        at = pl.ds(pl.multiple_of(side * COLS, COLS), COLS)
+        weight_load(wk_hbm, which, side).wait()
+        made = dot(tok[...], w[which, :, at], NN).astype(BF)
+        for n in range(per_side):
+            qkv[which, side * per_side + n] = made[:, n * HD : (n + 1) * HD]
 
     def x_copy(d, i):
         return remote(
@@ -232,37 +241,31 @@
         )
 
     def state(d, h):
-        if d == 0:
-            made = dot(qkv[2, h] * closec[...].astype(BF), qkv[1, h], TN)
-        else:
-            made = dot(g[h] * openc[...].astype(BF), qkv[0, h], TN)
-        for n in range(SPLIT):
-            st[d, h * SPLIT + n] = made[n * deep : (n + 1) * deep]
+        def hold(made):
+            for n in range(SPLIT):
+                st[d, h * SPLIT + n] = made[n * deep : (n + 1) * deep]
+
+        @pl.when(d == 0)
+        def _():
+            hold(dot(qkv[2, h] * closec[...].astype(BF), qkv[1, h], TN))
+
+        @pl.when(d == 1)
+        def _():
+            hold(dot(g[h] * openc[...].astype(BF), qkv[0, h], TN))
 
     def give(d):
-        for i in range(half):
+        @pl.loop(0, half)
+        def _(i):
             state(d, (1 - par) * half + i)
             for n in range(SPLIT):
                 x_copy(d, i * SPLIT + n).start()
 
-    def keys_values():
-        for n in (1, 2):
-            weight_loads[n].wait()
-            project(n)
-
-    def queries():
-        weight_loads[0].wait()
-        project(0)
-
-    token_load.wait()
-
-    @pl.when(turn == 0)
-    def _():
-        keys_values()
-
-    @pl.when(turn == 1)
-    def _():
-        queries()
+    for load in token_loads:
+        load.wait()
+
+    @pl.loop(0, (2 - turn) * sides)
+    def _(n):
+        project(jnp.where(turn == 0, 1 + n // sides, 0), n % sides)
 
     for load in g_loads:
         load.wait()
@@ -270,22 +273,23 @@
     pl.semaphore_wait(barrier, waits)
     flag_copy = remote(fl, xfl, fl_sem.at[0], fl_sem.at[1], {"ctx": mate})
     flag_copy.start()
-
-    @pl.when(turn == 0)
-    def _():
-        give(0)
-        queries()
-        give(1)
-
-    @pl.when(turn == 1)
-    def _():
-        give(1)
-        keys_values()
-        give(0)
-
-    for i in range(half):
-        state(0, par * half + i)
-        state(1, par * half + i)
+    give(turn)
+
+    @pl.loop(0, (1 + turn) * sides)
+    def _(n):
+        project(jnp.where(turn == 0, 0, 1 + n // sides), n % sides)
+
+    give(1 - turn)
+
+    @pl.loop(0, 2 * half)
+    def _(n):
+        state((n // half + turn) % 2, par * half + n % half)
+
+    below = (row_id < col_id).astype(F32).astype(BF)
+    before_row = dot(ends_row, below, NN)[0:1, :]
+    same = before_row == jnp.broadcast_to(count[:, 0:1], (rows, rows))
+    mask[...] = (same & (col_id <= row_id)).astype(F32).astype(BF)
+    flip[...] = (same & (row_id <= col_id)).astype(F32).astype(BF)
 
     def within(h):
         for start, stop in spans:
@@ -487,6 +491,7 @@
             pltpu.VMEM((rows, rows), BF),
             pltpu.VMEM((rows, HD), F32),
             pltpu.VMEM((rows, HD), F32),
+            pltpu.VMEM((rows, HD), F32),
             pltpu.VMEM((3, heads, rows, HD), F32),
             pltpu.VMEM((3, rows, inner), BF),
             pltpu.VMEM((2, heads * SPLIT, deep, HD), F32),
@@ -499,7 +504,7 @@
             pltpu.VMEM((2, *piece), F32),
             pltpu.VMEM(piece, F32),
             pltpu.VMEM(piece, F32),
-            dma((5 + heads,)),
+            dma((3 + heads + 3 * (inner // COLS),)),
             dma((2,)),
             dma((2, pieces)), dma((2, pieces)),
             dma((2, pieces)), dma((2, pieces)),
@@ -520,7 +525,7 @@
         rows, width = tokens_in.shape
         heads = w_query.shape[1] // HD
         fits = nt == 4 and nc % 2 == 0 and heads % 2 == 0 and rows <= 512
-        fits = fits and width % COLS == 0 and rows % 256 == 0
+        fits = fits and width % COLS == 0 and rows % 256 == 0 and w_query.shape[1] % COLS == 0
         call = functools.partial(fused_body, nc, nt) if fits else body
         return call(tokens_in, w_query, w_key, w_value, grad_out, trajectory_ends)
 

time: 53.1 us -> 54 us (1.017)
  Pallas kernels: 52.1 us -> 53 us
    pallas_call x1, Pallas kernels: 52.1 us -> 53 us  [fused_body(): pl.pallas_call(functools.partial(fused, nc, nt), out_shape=jax.ShapeDtype...]
where the time goes in v4:
time: 54 us; the launch traced here: 53.8 us
  Pallas kernels  53 us (98%)
  local copies, waits for them, and re-layouts  0.8 us (1%)
    pallas_call x1, Pallas kernels, fused_body(): pl.pallas_call(functools.partial(fused, nc, nt), out_shape=jax.ShapeDtype...  53 us

profile of v4, /device:TPU:0, one launch (start us, length us, event | category | flops | bytes accessed | tf_op | source)
XLA Modules:
  0.0 53.8 jit_solution(3253371840743302875)
XLA Ops:
  0.0 53.0 %shard_map.64 = bf16[128,2048]{1,0:T(8,128)(2,1)S(1)} custom-call(bf16[512,2048]{1,0:T(8,128)(2,1)} %tok_hbm.1, bf16[2048,512]{1,0:T(8,128)(2,1)} %wq_hbm.1, bf16[2048,512]{1,0:T(8,128)(2,1)} %wk_hbm.1, bf16[2048,512]{1,0:T(8,128)(2,1)} %wv_hbm.1, bf16[512,512]{1,0:T(8,128)(2,1)} %g_hbm.1, s32[1,512]{1,0:T(1,128)} %bitcast.1), custom_call_target="tpu_custom_call" | custom-call | tf_op jit(solution)/shard_map/pallas_call | solution.py:479
  53.0 0.8 %copy.8 = bf16[128,2048]{1,0:T(8,128)(2,1)} copy(bf16[128,2048]{1,0:T(8,128)(2,1)S(1)} %shard_map.64) | data formatting | bytes 1048576

commit v5 on v3

--- a/solution.py
+++ b/solution.py
@@ -113,7 +113,7 @@
 NT = ((1,), (1,))
 TN = ((0,), (0,))
 COLS = 256
-SPLIT = 2
+SPLIT = 4
 BF = jnp.bfloat16
 F32 = jnp.float32
 
@@ -354,16 +354,6 @@
             mine = jnp.where(first_here, into, inner).astype(BF)
             fin[d, par * half + i // SPLIT, place(i), :] = mine
 
-    at_end = (pair == 0) | (pair == pairs - 1)
-    early = jnp.where(at_end, 0, heads // 4)
-    late = jnp.where(at_end, heads - heads // 4, heads // 2)
-    flag_copy.wait_recv()
-    within_some(0, early)
-    carry(turn)
-    within_some(early, late)
-    carry(1 - turn)
-    within_some(late, heads)
-
     scale = 1.0 / HD
 
     def finish(d, h):
@@ -382,17 +372,43 @@
             dcat[1, :, at] = (scale * dk).astype(BF)
             dcat[2, :, at] = (scale * dv).astype(BF)
 
-    @pl.loop(0, 2 * half)
-    def _(n):
-        finish((n // half + turn) % 2, par * half + n % half)
-
-    for d in (turn, 1 - turn):
-        for i in range(half):
+    def finish_own(d):
+        @pl.loop(0, half)
+        def _(i):
+            finish(d, par * half + i)
+
+    def finish_mate(d):
+        @pl.loop(0, half)
+        def _(i):
             h = (1 - par) * half + i
-            for n in range(i * SPLIT, (i + 1) * SPLIT):
-                b_copy(d, n).wait_recv()
-                fin[d, h, place(n), :] = br[d, n].astype(BF)
+            for n in range(SPLIT):
+                b_copy(d, i * SPLIT + n).wait_recv()
+                fin[d, h, place(n), :] = br[d, i * SPLIT + n].astype(BF)
             finish(d, h)
+
+    at_end = (pair == 0) | (pair == pairs - 1)
+    early = jnp.where(at_end, 0, heads // 4)
+    late = jnp.where(at_end, heads, heads // 2)
+    flag_copy.wait_recv()
+    within_some(0, early)
+    carry(turn)
+    within_some(early, late)
+
+    @pl.when(at_end)
+    def _():
+        finish_own(turn)
+        finish_mate(turn)
+
+    carry(1 - turn)
+    within_some(late, heads)
+
+    @pl.when(jnp.logical_not(at_end))
+    def _():
+        finish_own(turn)
+        finish_mate(turn)
+
+    finish_own(1 - turn)
+    finish_mate(1 - turn)
 
     def rs_copy(part, j):
         return remote(

time: 53.1 us -> 53.1 us (level)
  no operation moved by 1% of the time
where the time goes in v5:
time: 53.1 us; the launch traced here: 52.9 us
  Pallas kernels  52.1 us (98%)
  local copies, waits for them, and re-layouts  0.8 us (2%)
    pallas_call x1, Pallas kernels, fused_body(): pl.pallas_call(functools.partial(fused, nc, nt), out_shape=jax.ShapeDtype...  52.1 us

profile of v5, /device:TPU:0, one launch (start us, length us, event | category | flops | bytes accessed | tf_op | source)
XLA Modules:
  0.0 52.9 jit_solution(13108172249301254972)
XLA Ops:
  0.0 52.1 %shard_map.64 = bf16[128,2048]{1,0:T(8,128)(2,1)S(1)} custom-call(bf16[512,2048]{1,0:T(8,128)(2,1)} %tok_hbm.1, bf16[2048,512]{1,0:T(8,128)(2,1)} %wq_hbm.1, bf16[2048,512]{1,0:T(8,128)(2,1)} %wk_hbm.1, bf16[2048,512]{1,0:T(8,128)(2,1)} %wv_hbm.1, bf16[512,512]{1,0:T(8,128)(2,1)} %g_hbm.1, s32[1,512]{1,0:T(1,128)} %bitcast.1), custom_call_target="tpu_custom_call" | custom-call | tf_op jit(solution)/shard_map/pallas_call | solution.py:491
  52.1 0.8 %copy.8 = bf16[128,2048]{1,0:T(8,128)(2,1)} copy(bf16[128,2048]{1,0:T(8,128)(2,1)S(1)} %shard_map.64) | data formatting | bytes 1048576

commit v6 on v5

--- a/solution.py
+++ b/solution.py
@@ -112,7 +112,7 @@
 NN = ((1,), (0,))
 NT = ((1,), (1,))
 TN = ((0,), (0,))
-COLS = 256
+COLS = 128
 SPLIT = 4
 BF = jnp.bfloat16
 F32 = jnp.float32

time: 53.1 us -> 53.6 us (level)
  no operation moved by 1% of the time
where the time goes in v6:
time: 53.6 us; the launch traced here: 53.4 us
  Pallas kernels  52.6 us (98%)
  local copies, waits for them, and re-layouts  0.8 us (1%)
    pallas_call x1, Pallas kernels, fused_body(): pl.pallas_call(functools.partial(fused, nc, nt), out_shape=jax.ShapeDtype...  52.6 us

profile of v6, /device:TPU:0, one launch (start us, length us, event | category | flops | bytes accessed | tf_op | source)
XLA Modules:
  0.0 53.4 jit_solution(6897461780606828849)
XLA Ops:
  0.0 52.6 %shard_map.64 = bf16[128,2048]{1,0:T(8,128)(2,1)S(1)} custom-call(bf16[512,2048]{1,0:T(8,128)(2,1)} %tok_hbm.1, bf16[2048,512]{1,0:T(8,128)(2,1)} %wq_hbm.1, bf16[2048,512]{1,0:T(8,128)(2,1)} %wk_hbm.1, bf16[2048,512]{1,0:T(8,128)(2,1)} %wv_hbm.1, bf16[512,512]{1,0:T(8,128)(2,1)} %g_hbm.1, s32[1,512]{1,0:T(1,128)} %bitcast.1), custom_call_target="tpu_custom_call" | custom-call | tf_op jit(solution)/shard_map/pallas_call | solution.py:491
  52.6 0.8 %copy.8 = bf16[128,2048]{1,0:T(8,128)(2,1)} copy(bf16[128,2048]{1,0:T(8,128)(2,1)S(1)} %shard_map.64) | data formatting | bytes 1048576
